TPU v7x, 32 devices: a whole 2x2x4 slice. The times are simulated.
32 devices in a mesh: groups: 2 (over y), blk: 8 (over z, core), width: 2 (over x).
Axes of the slice: x: 2, y: 2, z: 4, core: 2. Of those that a mesh axis runs over, the one named last changes fastest.
Arguments:
- tokens: bfloat16 [448, 4096], P(('groups', 'blk'), 'width'), parts along dimension 0, may hold values from -6 to 6
- grad_hidden: bfloat16 [448, 28672], P('groups', 'blk'), parts along dimension 0, may hold values from -2 to 2
- codes: bfloat16 [2, 4096, 28672], P(None, 'width', 'blk'), may hold values from -8 to 7, as said below
- scales: float32 [2, 32, 28672], P(None, 'width', 'blk'), may hold values from 0.0015625 to 0.015625
- pattern: int32 [224, 32], P('blk', 'width'), may hold values from 0 to 1
Outputs:
- grad_tokens: bfloat16 [448, 4096], P(('groups', 'blk'), 'width'), parts along dimension 0
- grad_log_scales: float32 [2, 64, 28672], P(None, ('groups', 'width'), 'blk'), parts along dimension 1
There are 2 independent parts, one for each index of `groups`. A program takes and returns all parts, laid end to end along the dimension named above; an argument that names none is the same for every part. Nothing has to cross between parts.
Inputs may be any that keep to these rules, and one draw needn't show every extreme that they name: `codes`: every code is a whole number.
All inputs are finite; a program needn't handle non-finite values.
Results may differ from a plain program's by a relative error of at most 0.017.
Values may be sent and summed in bfloat16 or wider, within the bound.
A program may use at most 192 MiB of HBM per device.

v0:
```python
import jax
import jax.numpy as jnp
from jax import lax
from jax.sharding import PartitionSpec as P


def dequantize(codes, scales, pattern):
    rows_tile = scales.shape[1]
    block = codes.shape[1] // rows_tile
    cols = codes.shape[2]
    mask = jnp.repeat(pattern.T, block, axis=1).astype(jnp.float32)
    factor = scales * mask[None]
    values = codes.astype(jnp.float32).reshape(2, rows_tile, block, cols) * factor[:, :, None, :]
    weight = values.reshape(codes.shape).astype(jnp.bfloat16)
    return (jnp.concatenate((weight[0], weight[1]), axis=1), factor)


def back_gates(hidden, upstream):
    half = upstream.shape[1]
    gate = hidden[:, :half]
    up = hidden[:, half:]
    grad_in = upstream.astype(jnp.float32)
    sig = jax.nn.sigmoid(gate)
    grad_gate = grad_in * up * sig * (1.0 + gate * (1.0 - sig))
    grad_up = grad_in * gate * sig
    return jnp.concatenate((grad_gate, grad_up), axis=1).astype(jnp.bfloat16)


def on_device(tokens, grad_hidden, codes, scales, pattern):
    cols_tile, rows_tile = pattern.shape
    block = codes.shape[1] // rows_tile
    slice_f = codes.shape[2]
    gathered = lax.all_gather(tokens, "blk", axis=0, tiled=True)
    joined, factor = dequantize(codes, scales, pattern)
    hidden = lax.psum(
        jnp.dot(gathered, joined, preferred_element_type=jnp.float32).astype(jnp.bfloat16), "width"
    ).astype(jnp.float32)
    grads = back_gates(hidden, grad_hidden)
    grad_tokens = lax.psum_scatter(
        lax.dot_general(
            grads, joined, (((1,), (1,)), ((), ())), preferred_element_type=jnp.float32
        ).astype(jnp.bfloat16),
        "blk",
        scatter_dimension=0,
        tiled=True,
    )
    weight_grad = lax.dot_general(
        gathered, grads, (((0,), (0,)), ((), ())), preferred_element_type=jnp.float32
    )
    codes_joined = jnp.concatenate((codes[0], codes[1]), axis=1).astype(jnp.float32)
    summed = (weight_grad * codes_joined).reshape(rows_tile, block, 2 * slice_f).sum(axis=1)
    factor_joined = jnp.concatenate((factor[0], factor[1]), axis=1)
    return (grad_tokens, (summed * factor_joined).reshape(rows_tile, 2, slice_f).transpose(1, 0, 2))


def solution(mesh):
    return jax.shard_map(
        on_device,
        mesh=mesh,
        in_specs=(
            P(("groups", "blk"), "width"),
            P("groups", "blk"),
            P(None, "width", "blk"),
            P(None, "width", "blk"),
            P("blk", "width"),
        ),
        out_specs=(P(("groups", "blk"), "width"), P(None, ("groups", "width"), "blk")),
        check_vma=False,
    )
```

profile of v0, /device:TPU:0, one launch (start us, length us, event | category | flops | bytes accessed | tf_op | source)
XLA Modules:
  0.0 245.3 jit_solution(5949424410235880979)
XLA Ops:
  7.2 0.0 all-reduce.4.cloned.1.call-start
  7.2 0.7 convert_bitcast_fusion
  7.9 0.1 broadcast_in_dim.2
  8.0 0.1 copy.16
  8.2 1.5 copy_multiply_fusion
  9.7 0.1 copy.11
  9.8 20.5 %fusion.1 = bf16[2,2048,3584]{2,1,0:T(8,128)(2,1)} fusion(bf16[2,2048,3584]{2,1,0:T(8,128)(2,1)} %param.7, f32[2,16,3584]{2,1,0:T(8,128)S(1)} %copy.11), kind=kLoop, calls=%fused_computation.3 | loop fusion | flops 44040192 | bytes 59179008 | tf_op jit(solution)/shard_map/convert_element_type | solution.py:14
  30.3 0.0 copy-start.4
  30.3 21.6 %slice_bitcast_fusion.1 = (bf16[2048,3584]{1,0:T(8,128)(2,1)}, bf16[2048,3584]{1,0:T(8,128)(2,1)}) fusion(bf16[2,2048,3584]{2,1,0:T(8,128)(2,1)} %fusion.1), kind=kLoop, calls=%fused_computation.8 | loop fusion | bytes 58720256 | tf_op jit(solution)/shard_map/squeeze | solution.py:15
  51.9 0.0 copy-done.4
  51.9 18.3 %all-gather = bf16[8,28,2048]{2,1,0:T(8,128)(2,1)S(1)} all-gather(bf16[1,28,2048]{2,1,0:T(8,128)(2,1)S(1)} %bitcast.40), channel_id=1, replica_groups=mesh['groups'=2,'blk'=8,'width'=2] {'blk'}, dimensions={0}, use_global_device_ids=true | all-gather | bytes 1032192 | tf_op jit(solution)/shard_map/all_gather | solution.py:33
  70.2 0.2 reshape.26
  70.4 0.0 copy-start.2
  70.4 0.0 copy-start.5
  70.4 14.7 %fusion.5 = bf16[224,7168]{1,0:T(8,128)(2,1)} fusion(bf16[224,2048]{1,0:T(8,128)(2,1)S(1)} %reshape.26, bf16[2048,3584]{1,0:T(8,128)(2,1)} %get-tuple-element.9, bf16[2048,3584]{1,0:T(8,128)(2,1)} %get-tuple-element.8), kind=kOutput, calls=%fused_computation.12 | convolution fusion | flops 6636994560 | bytes 33488896 | tf_op jit(solution)/shard_map/dot_general | solution.py:36
  85.2 0.0 copy-done.2
  85.2 0.0 all-reduce.4.cloned.1.call-update
  85.2 1.1 slice_bitcast_fusion.5
  86.2 0.0 copy-done.5
  86.2 0.6 dynamic-slice.4
  87.5 21.6 %slice_bitcast_fusion.3 = (bf16[2048,3584]{1,0:T(8,128)(2,1)}, bf16[2048,3584]{1,0:T(8,128)(2,1)}) fusion(bf16[2,2048,3584]{2,1,0:T(8,128)(2,1)} %param.7), kind=kLoop, calls=%fused_computation.10 | loop fusion | bytes 58720256 | tf_op jit(solution)/shard_map/squeeze | solution.py:50
  109.1 0.0 copy-start
  109.1 65.0 %all-reduce.4.cloned.1.call-done = bf16[224,7168]{1,0:T(8,128)(2,1)} async-done(((bf16[224,7168]{1,0:T(8,128)(2,1)}), bf16[224,7168]{1,0:T(8,128)(2,1)}) %all-reduce.4.cloned.1.call-update) | async-done | bytes 3211280 | tf_op jit(solution)/shard_map/psum | solution.py:35
  174.0 2.6 %convert_element_type.47 = f32[224,7168]{1,0:T(8,128)S(1)} convert(bf16[224,7168]{1,0:T(8,128)(2,1)} %all-reduce.4.cloned.1.call-done) | non-fusion elementwise | flops 1605632 | bytes 9633792 | tf_op jit(solution)/shard_map/convert_element_type | solution.py:37
  176.6 0.0 copy-done
  176.7 1.6 fusion.8
  178.2 0.0 copy-start.1
  178.2 1.1 copy-done.1
  179.4 0.0 copy-start.3
  179.4 14.2 %fusion.11 = bf16[224,2048]{1,0:T(8,128)(2,1)} fusion(bf16[2048,3584]{1,0:T(8,128)(2,1)} %get-tuple-element.9, bf16[2048,3584]{1,0:T(8,128)(2,1)} %get-tuple-element.8, bf16[224,3584]{1,0:T(8,128)(2,1)S(1)} %get-tuple-element.11, bf16[224,3584]{1,0:T(8,128)(2,1)S(1)} %get-tuple-element.10), kind=kOutput, calls=%fused_computation.22 | convolution fusion | flops 6642270208 | bytes 33488896 | tf_op jit(solution)/shard_map/dot_general | solution.py:40
  193.6 22.4 %fusion = bf16[32,2048]{1,0:T(8,128)(2,1)S(1)} fusion(bf16[224,2048]{1,0:T(8,128)(2,1)} %fusion.11), kind=kCustom, calls=%all-reduce-scatter | all-reduce-scatter fusion | flops 524289 | bytes 1049088
  216.0 0.7 slice.38
  216.7 1.9 collective-permute-start
  218.7 0.0 copy-done.3
  218.7 14.2 %bitcast_reduce_fusion = f32[16,7168]{1,0:T(8,128)} fusion(bf16[224,2048]{1,0:T(8,128)(2,1)S(1)} %copy-done.3, bf16[2048,3584]{1,0:T(8,128)(2,1)} %get-tuple-element.7, bf16[2048,3584]{1,0:T(8,128)(2,1)} %get-tuple-element.6, bf16[224,3584]{1,0:T(8,128)(2,1)} %copy-done.1, bf16[224,3584]{1,0:T(8,128)(2,1)S(1)} %get-tuple-element.10), kind=kOutput, calls=%fused_computation | convolution fusion | flops 6671056896 | bytes 33947648 | tf_op jit(solution)/shard_map/dot_general | solution.py:47
  232.9 1.4 reduce_sum.12
  234.3 1.4 fusion.12
  235.8 0.9 copy.12
  236.6 0.0 collective-permute-done
  236.6 1.2 concatenate.24
  237.8 0.7 constant_dynamic-slice_fusion
Async XLA Ops:
  7.2 166.8 %all-reduce.4.cloned.1.call-start = ((), (), s32[]{:S(2)}) async-start(), calls=%async_computation | async-start | bytes 6422528 | tf_op jit(solution)/shard_map/psum | solution.py:35
  30.3 21.6 %copy-start.4 = (bf16[28,2048]{1,0:T(8,128)(2,1)S(1)}, bf16[28,2048]{1,0:T(8,128)(2,1)}, u32[]{:S(2)}) copy-start(bf16[28,2048]{1,0:T(8,128)(2,1)} %param.5) | copy-start | bytes 344068
  70.4 14.8 %copy-start.2 = (bf16[224,2048]{1,0:T(8,128)(2,1)}, bf16[224,2048]{1,0:T(8,128)(2,1)S(1)}, u32[]{:S(2)}) copy-start(bf16[224,2048]{1,0:T(8,128)(2,1)S(1)} %reshape.26) | copy-start | bytes 2752516
  70.4 15.8 %copy-start.5 = (u32[32]{0:T(128)S(1)}, u32[32]{0:T(128)}, u32[]{:S(2)}) copy-start(u32[32]{0:T(128)} %constant.8) | copy-start | bytes 388
  109.1 67.6 %copy-start = (bf16[224,3584]{1,0:T(8,128)(2,1)S(1)}, bf16[224,3584]{1,0:T(8,128)(2,1)}, u32[]{:S(2)}) copy-start(bf16[224,3584]{1,0:T(8,128)(2,1)} %param.6) | copy-start | bytes 4816900
  178.2 1.2 copy-start.1
  179.4 39.3 %copy-start.3 = (bf16[224,2048]{1,0:T(8,128)(2,1)S(1)}, bf16[224,2048]{1,0:T(8,128)(2,1)}, u32[]{:S(2)}) copy-start(bf16[224,2048]{1,0:T(8,128)(2,1)} %copy-done.2) | copy-start | bytes 2752516
  216.7 19.9 %collective-permute-start = (bf16[28,2048]{1,0:T(8,128)(2,1)}, bf16[28,2048]{1,0:T(8,128)(2,1)}, u32[]{:S(2)}, u32[]{:S(2)}) collective-permute-start(bf16[28,2048]{1,0:T(8,128)(2,1)} %slice.38), channel_id=1, source_target_pairs={{0,2},{2,4},{4,6},{6,8},{8,10},{10,12},{12,14},{1,3},{3,5},{5,7},{... | collective-permute-start | bytes 344072
Sparse Core Ops, SparseCore 0:
  85.3 88.6 all-reduce.3
where the time goes:
time: 246 us; the launch traced here: 245 us
  waiting for transfers between devices  65 us (26%)
  local copies, waits for them, and re-layouts  51.3 us (21%)
  matrix products  43.2 us (18%)
  blocking collectives  40.8 us (17%)
  other arithmetic  28.4 us (12%)
  between operations  14.8 us (6%)
    psum x1, waiting for transfers between devices, on_device(): lax.psum(jnp.dot(gathered, joined, preferred_element_type=jnp.float32).as...  65 us
    unnamed x1, blocking collectives  22.4 us
    squeeze x1, local copies, waits for them, and re-layouts, on_device(): codes[0]  21.6 us
    squeeze x1, local copies, waits for them, and re-layouts, dequantize(): return (jnp.concatenate((weight[0], weight[1]), axis=1), factor)  21.6 us
    convert_element_type x1, other arithmetic, dequantize(): weight = values.reshape(codes.shape).astype(jnp.bfloat16)  20.5 us
    all_gather x1, blocking collectives, on_device(): gathered = lax.all_gather(tokens, 'blk', axis=0, tiled=True)  18.3 us
    dot_general x1, matrix products, on_device(): jnp.dot(gathered, joined, preferred_element_type=jnp.float32)  14.7 us
    dot_general x1, matrix products, on_device(): lax.dot_general(gathered, grads, (((0,), (0,)), ((), ())), preferred_elem...  14.2 us
  transfers between devices with their start and end apart: 2, of which 1 were waited for; matrix products, arithmetic and copies ran while one was open for 17% of the time, Pallas kernels for 0%

commit v1 on v0

--- a/solution.py
+++ b/solution.py
@@ -30,7 +30,12 @@
     cols_tile, rows_tile = pattern.shape
     block = codes.shape[1] // rows_tile
     slice_f = codes.shape[2]
-    gathered = lax.all_gather(tokens, "blk", axis=0, tiled=True)
+    ring = [tokens]
+    for hop in range(7):
+        ring.append(lax.ppermute(ring[-1], "blk", [(dev, (dev + 1) % 8) for dev in range(8)]))
+    gathered = jnp.roll(
+        jnp.concatenate(ring[::-1], axis=0), (lax.axis_index("blk") + 1) * ring[0].shape[0], axis=0
+    )
     joined, factor = dequantize(codes, scales, pattern)
     hidden = lax.psum(
         jnp.dot(gathered, joined, preferred_element_type=jnp.float32).astype(jnp.bfloat16), "width"

time: 246 us -> 257 us (1.045)
  waiting for transfers between devices: 65 us -> 96.1 us
  blocking collectives: 40.8 us -> 21.9 us
    ppermute x0 -> x7, waiting for transfers between devices: none -> 30.7 us  [on_device(): lax.ppermute(ring[-1], 'blk', [(dev, (dev + 1) % 8) for dev in range(8)])]
    all_gather x1 -> x0, blocking collectives: 18.3 us -> none  [on_device(): gathered = lax.all_gather(tokens, 'blk', axis=0, tiled=True)]
    unnamed x19 -> x20, local copies, waits for them, and re-layouts: 5.47 us -> 5.12 us
  transfers between devices with their start and end apart: 2 -> 9, of which waited for: 1 -> 6; matrix products, arithmetic and copies ran while one was open for 17% -> 32% of each run, Pallas kernels for 0% -> 0%
where the time goes in v1:
time: 257 us
  waiting for transfers between devices  96.1 us (37%)
  local copies, waits for them, and re-layouts  51.6 us (20%)
  matrix products  42 us (16%)
  other arithmetic  27.5 us (11%)
  blocking collectives  21.9 us (9%)
  between operations  14.9 us (6%)
    psum x1, waiting for transfers between devices, on_device(): lax.psum(jnp.dot(gathered, joined, preferred_element_type=jnp.float32).as...  65.4 us
    ppermute x7, waiting for transfers between devices, on_device(): lax.ppermute(ring[-1], 'blk', [(dev, (dev + 1) % 8) for dev in range(8)])  30.7 us
    unnamed x1, blocking collectives  21.9 us
    squeeze x1, local copies, waits for them, and re-layouts, on_device(): codes[0]  21.6 us
    squeeze x1, local copies, waits for them, and re-layouts, dequantize(): return (jnp.concatenate((weight[0], weight[1]), axis=1), factor)  21.4 us
    convert_element_type x1, other arithmetic, dequantize(): weight = values.reshape(codes.shape).astype(jnp.bfloat16)  20.5 us
    dot_general x1, matrix products, on_device(): jnp.dot(gathered, joined, preferred_element_type=jnp.float32)  14.7 us
    dot_general x1, matrix products, on_device(): lax.dot_general(gathered, grads, (((0,), (0,)), ((), ())), preferred_elem...  13.9 us
  transfers between devices with their start and end apart: 9, of which 6 were waited for; matrix products, arithmetic and copies ran while one was open for 32% of the time, Pallas kernels for 0%

profile of v1, /device:TPU:0, one launch (start us, length us, event | category | flops | bytes accessed | tf_op | source)
XLA Modules:
  0.0 256.6 jit_solution(14019820833542995489)
XLA Ops:
  7.2 0.0 all-reduce.4.cloned.1.call-start
  7.2 0.5 collective-permute-start
  7.7 6.9 %collective-permute-done = bf16[28,2048]{1,0:T(8,128)(2,1)S(1)} collective-permute-done((bf16[28,2048]{1,0:T(8,128)(2,1)}, bf16[28,2048]{1,0:T(8,128)(2,1)S(1)}, u32[]{:S(2)}, u32[]{:S(2)}) %collective-permute-start) | collective-permute-done | bytes 114720 | tf_op jit(solution)/shard_map/ppermute | solution.py:35
  14.6 0.0 collective-permute-start.1
  14.6 6.2 %collective-permute-done.1 = bf16[28,2048]{1,0:T(8,128)(2,1)S(1)} collective-permute-done((bf16[28,2048]{1,0:T(8,128)(2,1)S(1)}, bf16[28,2048]{1,0:T(8,128)(2,1)S(1)}, u32[]{:S(2)}, u32[]{:S(2)}) %collective-permute-start.1) | collective-permute-done | bytes 114720 | tf_op jit(solution)/shard_map/ppermute | solution.py:35
  20.8 0.0 collective-permute-start.2
  20.8 6.2 %collective-permute-done.2 = bf16[28,2048]{1,0:T(8,128)(2,1)S(1)} collective-permute-done((bf16[28,2048]{1,0:T(8,128)(2,1)S(1)}, bf16[28,2048]{1,0:T(8,128)(2,1)S(1)}, u32[]{:S(2)}, u32[]{:S(2)}) %collective-permute-start.2) | collective-permute-done | bytes 114720 | tf_op jit(solution)/shard_map/ppermute | solution.py:35
  27.0 0.0 collective-permute-start.3
  27.0 6.2 %collective-permute-done.3 = bf16[28,2048]{1,0:T(8,128)(2,1)S(1)} collective-permute-done((bf16[28,2048]{1,0:T(8,128)(2,1)S(1)}, bf16[28,2048]{1,0:T(8,128)(2,1)S(1)}, u32[]{:S(2)}, u32[]{:S(2)}) %collective-permute-start.3) | collective-permute-done | bytes 114720 | tf_op jit(solution)/shard_map/ppermute | solution.py:35
  33.2 0.0 collective-permute-start.4
  33.2 0.7 convert_bitcast_fusion
  33.9 0.1 broadcast_in_dim.2
  34.0 0.1 copy.16
  34.2 5.2 %collective-permute-done.4 = bf16[28,2048]{1,0:T(8,128)(2,1)S(1)} collective-permute-done((bf16[28,2048]{1,0:T(8,128)(2,1)S(1)}, bf16[28,2048]{1,0:T(8,128)(2,1)S(1)}, u32[]{:S(2)}, u32[]{:S(2)}) %collective-permute-start.4) | collective-permute-done | bytes 114720 | tf_op jit(solution)/shard_map/ppermute | solution.py:35
  39.4 0.0 collective-permute-start.5
  39.4 1.5 copy_multiply_fusion
  40.9 0.1 copy.11
  41.0 20.5 %fusion.1 = bf16[2,2048,3584]{2,1,0:T(8,128)(2,1)} fusion(bf16[2,2048,3584]{2,1,0:T(8,128)(2,1)} %param.7, f32[2,16,3584]{2,1,0:T(8,128)S(1)} %copy.11), kind=kLoop, calls=%fused_computation.2 | loop fusion | flops 44040192 | bytes 59179008 | tf_op jit(solution)/shard_map/convert_element_type | solution.py:14
  61.4 0.0 copy-start.5
  61.4 0.0 collective-permute-done.5
  61.5 0.1 collective-permute-start.6
  61.5 21.4 %slice_bitcast_fusion.1 = (bf16[2048,3584]{1,0:T(8,128)(2,1)}, bf16[2048,3584]{1,0:T(8,128)(2,1)}) fusion(bf16[2,2048,3584]{2,1,0:T(8,128)(2,1)} %fusion.1), kind=kLoop, calls=%fused_computation.8 | loop fusion | bytes 58720256 | tf_op jit(solution)/shard_map/squeeze | solution.py:15
  82.9 0.0 collective-permute-done.6
  82.9 0.0 copy-done.5
  82.9 1.8 concatenate.24
  84.7 0.0 copy-start.6
  84.7 14.7 %fusion.4 = bf16[224,7168]{1,0:T(8,128)(2,1)} fusion(bf16[2048,3584]{1,0:T(8,128)(2,1)} %get-tuple-element.9, bf16[2048,3584]{1,0:T(8,128)(2,1)} %get-tuple-element.8, bf16[448,2048]{1,0:T(8,128)(2,1)S(1)} %concatenate.24, s32[]{:T(128)S(6)} %select_n.14), kind=kOutput, calls=%fused_computation.11 | convolution fusion | flops 6636994560 | bytes 33488900 | tf_op jit(solution)/shard_map/dot_general | solution.py:41
  99.4 0.0 all-reduce.4.cloned.1.call-update
  99.4 1.1 slice_bitcast_fusion.5
  100.5 0.0 copy-done.6
  100.5 0.6 dynamic-slice.4
  101.8 21.6 %slice_bitcast_fusion.3 = (bf16[2048,3584]{1,0:T(8,128)(2,1)}, bf16[2048,3584]{1,0:T(8,128)(2,1)}) fusion(bf16[2,2048,3584]{2,1,0:T(8,128)(2,1)} %param.7), kind=kLoop, calls=%fused_computation.10 | loop fusion | bytes 58720256 | tf_op jit(solution)/shard_map/squeeze | solution.py:55
  123.4 65.4 %all-reduce.4.cloned.1.call-done = bf16[224,7168]{1,0:T(8,128)(2,1)} async-done(((bf16[224,7168]{1,0:T(8,128)(2,1)}), bf16[224,7168]{1,0:T(8,128)(2,1)}) %all-reduce.4.cloned.1.call-update) | async-done | bytes 3211280 | tf_op jit(solution)/shard_map/psum | solution.py:40
  188.8 0.0 copy-start
  188.8 2.8 %convert_element_type.43 = f32[224,7168]{1,0:T(8,128)S(1)} convert(bf16[224,7168]{1,0:T(8,128)(2,1)} %all-reduce.4.cloned.1.call-done) | non-fusion elementwise | flops 1605632 | bytes 9633792 | tf_op jit(solution)/shard_map/convert_element_type | solution.py:42
  191.6 0.0 copy-done
  191.6 1.5 fusion.7
  193.1 0.0 copy-start.1
  193.2 0.0 copy-start.2
  193.2 1.1 copy-done.1
  194.3 0.5 copy-done.2
  194.8 13.4 %fusion.10 = bf16[224,2048]{1,0:T(8,128)(2,1)S(1)} fusion(bf16[2048,3584]{1,0:T(8,128)(2,1)} %get-tuple-element.9, bf16[2048,3584]{1,0:T(8,128)(2,1)} %get-tuple-element.8, bf16[224,3584]{1,0:T(8,128)(2,1)S(1)} %get-tuple-element.11, bf16[224,3584]{1,0:T(8,128)(2,1)S(1)} %get-tuple-element.10), kind=kOutput, calls=%fused_computation.21 | convolution fusion | flops 6642270208 | bytes 33488896 | tf_op jit(solution)/shard_map/dot_general | solution.py:45
  208.2 21.9 %fusion = bf16[32,2048]{1,0:T(8,128)(2,1)S(1)} fusion(bf16[224,2048]{1,0:T(8,128)(2,1)S(1)} %fusion.10), kind=kCustom, calls=%all-reduce-scatter | all-reduce-scatter fusion | flops 524289 | bytes 1049088
  230.2 1.9 collective-permute-start.7
  232.1 0.0 copy-start.3
  232.1 0.0 copy-start.4
  232.1 13.9 %bitcast_reduce_fusion = f32[16,7168]{1,0:T(8,128)S(1)} fusion(bf16[2048,3584]{1,0:T(8,128)(2,1)} %get-tuple-element.7, bf16[2048,3584]{1,0:T(8,128)(2,1)} %get-tuple-element.6, bf16[224,3584]{1,0:T(8,128)(2,1)} %copy-done.2, bf16[224,3584]{1,0:T(8,128)(2,1)} %copy-done.1, bf16[448,2048]{1,0:T(8,128)(2,1)S(1)} %concatenate.24, s32[]{:T(128)S(6)} %select_n.14), kind=kOutput, calls=%fused_computation | convolution fusion | flops 6671056896 | bytes 33947652 | tf_op jit(solution)/shard_map/dot_general | solution.py:52
  246.1 0.4 reduce_sum.12
  246.5 0.0 copy-done.3
  246.5 0.0 copy-done.4
  246.5 0.5 fusion.13
  247.0 0.9 copy.12
  247.8 0.0 collective-permute-done.7
  247.8 1.2 concatenate.31
  249.0 0.7 constant_dynamic-slice_fusion
  (1 shorter events, 0.0 us)
Async XLA Ops:
  7.2 181.7 %all-reduce.4.cloned.1.call-start = ((), (), s32[]{:S(2)}) async-start(), calls=%async_computation | async-start | bytes 6422528 | tf_op jit(solution)/shard_map/psum | solution.py:40
  7.2 7.4 %collective-permute-start = (bf16[28,2048]{1,0:T(8,128)(2,1)}, bf16[28,2048]{1,0:T(8,128)(2,1)S(1)}, u32[]{:S(2)}, u32[]{:S(2)}) collective-permute-start(bf16[28,2048]{1,0:T(8,128)(2,1)} %param.5), channel_id=1, source_target_pairs={{0,2},{2,4},{4,6},{6,8},{8,10},{10,12},{12,14},{14,0},{1,3},{3,5},... | collective-permute-start | bytes 344072 | tf_op jit(solution)/shard_map/ppermute | solution.py:35
  14.6 6.2 %collective-permute-start.1 = (bf16[28,2048]{1,0:T(8,128)(2,1)S(1)}, bf16[28,2048]{1,0:T(8,128)(2,1)S(1)}, u32[]{:S(2)}, u32[]{:S(2)}) collective-permute-start(bf16[28,2048]{1,0:T(8,128)(2,1)S(1)} %collective-permute-done), channel_id=1, source_target_pairs={{0,2},{2,4},{4,6},{6,8},{8,10},{10,12},{12,14},{14,0},{1,3},{3,5},... | collective-permute-start | bytes 344072 | tf_op jit(solution)/shard_map/ppermute | solution.py:35
  20.8 6.2 %collective-permute-start.2 = (bf16[28,2048]{1,0:T(8,128)(2,1)S(1)}, bf16[28,2048]{1,0:T(8,128)(2,1)S(1)}, u32[]{:S(2)}, u32[]{:S(2)}) collective-permute-start(bf16[28,2048]{1,0:T(8,128)(2,1)S(1)} %collective-permute-done.1), channel_id=1, source_target_pairs={{0,2},{2,4},{4,6},{6,8},{8,10},{10,12},{12,14},{14,0},{1,3},{3,5},... | collective-permute-start | bytes 344072 | tf_op jit(solution)/shard_map/ppermute | solution.py:35
  27.0 6.2 %collective-permute-start.3 = (bf16[28,2048]{1,0:T(8,128)(2,1)S(1)}, bf16[28,2048]{1,0:T(8,128)(2,1)S(1)}, u32[]{:S(2)}, u32[]{:S(2)}) collective-permute-start(bf16[28,2048]{1,0:T(8,128)(2,1)S(1)} %collective-permute-done.2), channel_id=1, source_target_pairs={{0,2},{2,4},{4,6},{6,8},{8,10},{10,12},{12,14},{14,0},{1,3},{3,5},... | collective-permute-start | bytes 344072 | tf_op jit(solution)/shard_map/ppermute | solution.py:35
  33.2 6.2 %collective-permute-start.4 = (bf16[28,2048]{1,0:T(8,128)(2,1)S(1)}, bf16[28,2048]{1,0:T(8,128)(2,1)S(1)}, u32[]{:S(2)}, u32[]{:S(2)}) collective-permute-start(bf16[28,2048]{1,0:T(8,128)(2,1)S(1)} %collective-permute-done.3), channel_id=1, source_target_pairs={{0,2},{2,4},{4,6},{6,8},{8,10},{10,12},{12,14},{14,0},{1,3},{3,5},... | collective-permute-start | bytes 344072 | tf_op jit(solution)/shard_map/ppermute | solution.py:35
  39.4 22.1 %collective-permute-start.5 = (bf16[28,2048]{1,0:T(8,128)(2,1)S(1)}, bf16[28,2048]{1,0:T(8,128)(2,1)S(1)}, u32[]{:S(2)}, u32[]{:S(2)}) collective-permute-start(bf16[28,2048]{1,0:T(8,128)(2,1)S(1)} %collective-permute-done.4), channel_id=1, source_target_pairs={{0,2},{2,4},{4,6},{6,8},{8,10},{10,12},{12,14},{14,0},{1,3},{3,5},... | collective-permute-start | bytes 344072 | tf_op jit(solution)/shard_map/ppermute | solution.py:35
  61.4 21.4 %copy-start.5 = (bf16[28,2048]{1,0:T(8,128)(2,1)S(1)}, bf16[28,2048]{1,0:T(8,128)(2,1)}, u32[]{:S(2)}) copy-start(bf16[28,2048]{1,0:T(8,128)(2,1)} %param.5) | copy-start | bytes 344068
  61.5 21.4 %collective-permute-start.6 = (bf16[28,2048]{1,0:T(8,128)(2,1)S(1)}, bf16[28,2048]{1,0:T(8,128)(2,1)S(1)}, u32[]{:S(2)}, u32[]{:S(2)}) collective-permute-start(bf16[28,2048]{1,0:T(8,128)(2,1)S(1)} %collective-permute-done.5), channel_id=1, source_target_pairs={{0,2},{2,4},{4,6},{6,8},{8,10},{10,12},{12,14},{14,0},{1,3},{3,5},... | collective-permute-start | bytes 344072 | tf_op jit(solution)/shard_map/ppermute | solution.py:35
  84.7 15.8 %copy-start.6 = (u32[32]{0:T(128)S(1)}, u32[32]{0:T(128)}, u32[]{:S(2)}) copy-start(u32[32]{0:T(128)} %constant.37) | copy-start | bytes 388
  188.8 2.8 %copy-start = (bf16[224,3584]{1,0:T(8,128)(2,1)S(1)}, bf16[224,3584]{1,0:T(8,128)(2,1)}, u32[]{:S(2)}) copy-start(bf16[224,3584]{1,0:T(8,128)(2,1)} %param.6) | copy-start | bytes 4816900
  193.1 1.1 copy-start.1
  193.2 1.6 copy-start.2
  230.2 17.7 %collective-permute-start.7 = (bf16[28,2048]{1,0:T(8,128)(2,1)S(1)}, bf16[28,2048]{1,0:T(8,128)(2,1)}, u32[]{:S(2)}, u32[]{:S(2)}) collective-permute-start(bf16[28,2048]{1,0:T(8,128)(2,1)S(1)} %slice.38), channel_id=1, source_target_pairs={{0,2},{2,4},{4,6},{6,8},{8,10},{10,12},{12,14},{1,3},{3,5},{5,7},{... | collective-permute-start | bytes 344072
  232.1 14.3 %copy-start.3 = (f32[16,1,3584]{2,1,0:T(1,128)S(1)}, f32[16,1,3584]{2,1,0:T(1,128)}, u32[]{:S(2)}) copy-start(f32[16,1,3584]{2,1,0:T(1,128)} %get-tuple-element.12) | copy-start | bytes 688132
  232.1 14.4 %copy-start.4 = (f32[16,1,3584]{2,1,0:T(1,128)S(1)}, f32[16,1,3584]{2,1,0:T(1,128)}, u32[]{:S(2)}) copy-start(f32[16,1,3584]{2,1,0:T(1,128)} %get-tuple-element.13) | copy-start | bytes 688132
Sparse Core Ops, SparseCore 0:
  99.5 89.2 all-reduce.3
